TPU v7x, 256 devices: a whole 4x4x8 slice. The times are simulated.
256 devices in a mesh: dp: 16 (over y, x), vocab: 16 (over z, core).
Axes of the slice: x: 4, y: 4, z: 8, core: 2. Of those that a mesh axis runs over, the one named last changes fastest.
Arguments:
- hidden: bfloat16 [768, 4096], P(('dp', 'vocab')), may hold values from -240 to 240
- head_weight: bfloat16 [4096, 163840], P(None, ('dp', 'vocab')), may hold values from -0.40625 to 0.40625
- targets: int32 [768], P(('dp', 'vocab')), may hold values from 0 to 163839, as said below
- image_mask: int32 [768], P(('dp', 'vocab')), may hold values from 0 to 1
- lengths: int32 [16], replicated, may hold values from 12 to 48, as said below
- ref_logps: float32 [16], replicated, may hold values from -18 to -13
- pairing: int32 [16], replicated, may hold values from 0 to 15, each once
Outputs:
- grad_hidden: bfloat16 [768, 4096], P(('dp', 'vocab'))
- grad_head: bfloat16 [4096, 163840], P(None, ('dp', 'vocab'))
- mean_loss: float32 [], replicated
Inputs may be any that keep to these rules, and one draw needn't show every extreme that they name: `targets`: each token's target lies in its modality's columns: at least 131072 where image_mask is 1, below it where image_mask is 0. `lengths`: some window is full.
All inputs are finite; a program needn't handle non-finite values.
Results may differ from a plain program's by a relative error of at most 0.0067.
Values may be sent and summed in bfloat16 or wider, within the bound.
No kernel may reach another device: no remote copies, remote signals or barrier semaphores. Data moves between devices by JAX's collectives and lax.ppermute only.
A program may use at most 128 MiB of HBM per device.

v0:
```python
import jax
import jax.numpy as jnp
from jax import lax
from jax.sharding import PartitionSpec as P

V = 163840
CODES = 32768
WIN = 48


NEG = -1e30
BETA = 1.0
LOSS_SCALE = 4096.0


def preference(token_lp, lengths, ref_logps, pairing):
    groups = lengths.shape[0]
    per_group = token_lp.reshape(groups, WIN)
    is_valid = jnp.arange(WIN, dtype=jnp.int32)[None, :] < lengths[:, None]
    token_count = lengths.astype(jnp.float32)
    policy = jnp.sum(jnp.where(is_valid, per_group, 0.0), axis=1) / token_count
    shifted = policy - ref_logps
    members = jnp.arange(groups, dtype=jnp.int32)
    chosen = (pairing[0::2][:, None] == members[None, :]).astype(jnp.float32)
    rejected = (pairing[1::2][:, None] == members[None, :]).astype(jnp.float32)
    pair_signs = chosen - rejected
    margin = BETA * jnp.sum(pair_signs * shifted[None, :], axis=1)
    mean_loss = jnp.mean(jax.nn.softplus(-margin))
    pair_weight = -LOSS_SCALE * BETA * jax.nn.sigmoid(-margin) / margin.shape[0]
    group_weight = jnp.sum(pair_weight[:, None] * pair_signs, axis=0) / token_count
    token_weight = jnp.where(is_valid, group_weight[:, None], 0.0).reshape(-1)
    return (mean_loss, token_weight)


def local(hidden, head_weight, targets, image_mask, lengths, ref_logps, pairing):
    gathered, all_targets, all_images = (
        lax.all_gather(hidden, ("dp", "vocab"), axis=0, tiled=True),
        lax.all_gather(targets, ("dp", "vocab"), axis=0, tiled=True),
        lax.all_gather(image_mask, ("dp", "vocab"), axis=0, tiled=True),
    )
    columns = head_weight.shape[1]
    first_column = lax.axis_index(("dp", "vocab")) * columns
    column_ids = first_column + jnp.arange(columns, dtype=jnp.int32)
    code_column = column_ids >= V - CODES
    logits = jnp.dot(gathered, head_weight, preferred_element_type=jnp.float32)
    in_range = (all_images[:, None] == 1) == code_column[None, :]
    masked = jnp.where(in_range, logits, NEG)
    is_target = column_ids[None, :] == all_targets[:, None]
    target_part = jnp.sum(jnp.where(is_target, logits, 0.0), axis=1)
    row_peak = lax.pmax(jnp.max(masked, axis=1), ("dp", "vocab"))
    local_total = jnp.sum(jnp.where(in_range, jnp.exp(masked - row_peak[:, None]), 0.0), axis=1)
    row_total, target_logit = lax.psum((local_total, target_part), ("dp", "vocab"))
    log_norm = row_peak + jnp.log(row_total)
    token_lp = target_logit - log_norm
    mean_loss, token_weight = preference(token_lp, lengths, ref_logps, pairing)
    row_probs = jnp.where(in_range, jnp.exp(logits - log_norm[:, None]), 0.0)
    logit_grad = (token_weight[:, None] * (is_target.astype(jnp.float32) - row_probs)).astype(
        jnp.bfloat16
    )
    grad_head = lax.dot_general(
        gathered, logit_grad, (((0,), (0,)), ((), ())), preferred_element_type=jnp.float32
    ).astype(jnp.bfloat16)
    grad_hidden = lax.psum_scatter(
        lax.dot_general(
            logit_grad, head_weight, (((1,), (1,)), ((), ())), preferred_element_type=jnp.float32
        ),
        ("dp", "vocab"),
        scatter_dimension=0,
        tiled=True,
    )
    return (grad_hidden.astype(jnp.bfloat16), grad_head, mean_loss)


def solution(mesh):
    return jax.shard_map(
        local,
        mesh=mesh,
        in_specs=(
            P(("dp", "vocab"), None),
            P(None, ("dp", "vocab")),
            P(("dp", "vocab")),
            P(("dp", "vocab")),
            P(),
            P(),
            P(),
        ),
        out_specs=(P(("dp", "vocab"), None), P(None, ("dp", "vocab")), P()),
        check_vma=False,
    )
```

profile of v0, /device:TPU:1, one launch (start us, length us, event | category | flops | bytes accessed | tf_op | source)
XLA Modules:
  0.0 501.5 jit_solution(10985688407232349578)
XLA Ops:
  7.2 0.0 all-gather.3.cloned.1.call-start
  7.2 0.7 all-gather.3.cloned.1.call-update
  7.9 0.7 slice.6
  8.7 0.7 slice.7
  9.4 0.9 dynamic-update-slice
  10.3 0.8 dynamic-update-slice.1
  11.1 82.1 %all-reduce.3 = (s32[768]{0:T(1024)S(1)}, s32[768]{0:T(1024)S(1)}) all-reduce(s32[768]{0:T(1024)S(1)} %dynamic-update-slice.1, s32[768]{0:T(1024)S(1)} %dynamic-update-slice), channel_id=1, replica_groups=mesh['dp'=16,'vocab'=16] {'dp','vocab'}, use_global_device_ids=true, to_apply=%add.1 | all-reduce | flops 1536 | bytes 12288
  93.3 41.0 %all-gather.3.cloned.1.call-done = bf16[256,3,4096]{2,1,0:T(4,128)(2,1)} async-done(((bf16[1,3,4096]{2,1,0:T(4,128)(2,1)}), bf16[256,3,4096]{2,1,0:T(4,128)(2,1)}) %all-gather.3.cloned.1.call-update) | async-done | bytes 6291472 | tf_op jit(solution)/shard_map/all_gather | solution.py:37
  134.2 13.7 %reshape.61 = bf16[768,4096]{1,0:T(8,128)(2,1)} reshape(bf16[256,3,4096]{2,1,0:T(4,128)(2,1)} %all-gather.3.cloned.1.call-done) | data formatting | bytes 12582912
  147.9 9.2 %fusion.6 = (f32[768]{0:T(1024)S(1)}, f32[768,640]{0,1:T(8,128)S(1)}) fusion(pred[768]{0:T(1024)(128)(4,1)S(1)} %broadcast_compare_fusion.1, pred[640]{0:T(1024)(128)(4,1)S(1)} %broadcast_compare_fusion, bf16[768,4096]{1,0:T(8,128)(2,1)} %reshape.61, bf16[4096,640]{1,0:T(8,128)(2,1)} %param.8), kind=kOutput, calls=%fused_computation.12 | convolution fusion | flops 4028005632 | bytes 13504896 | tf_op jit(solution)/shard_map/dot_general | solution.py:45
  157.1 0.0 copy-start
  157.2 0.0 copy-start.1
  157.2 74.5 %pmax.7 = f32[768]{0:T(1024)S(1)} all-reduce(f32[768]{0:T(1024)S(1)} %get-tuple-element.25), channel_id=1, replica_groups=mesh['dp'=16,'vocab'=16] {'dp','vocab'}, use_global_device_ids=true, to_apply=%region_3.4 | all-reduce | flops 768 | bytes 6144 | tf_op jit(solution)/shard_map/pmax | solution.py:50
  231.6 0.7 fusion.1
  232.4 73.7 %all-reduce.4 = (f32[768]{0:T(1024)S(1)}, f32[768]{0:T(1024)S(1)}) all-reduce(f32[768]{0:T(1024)S(1)} %get-tuple-element.16, f32[768]{0:T(1024)S(1)} %get-tuple-element.15), channel_id=1, replica_groups=mesh['dp'=16,'vocab'=16] {'dp','vocab'}, use_global_device_ids=true, to_apply=%region_5.6 | all-reduce | flops 1536 | bytes 12288 | tf_op jit(solution)/shard_map/psum | solution.py:52
  306.1 0.1 reshape.55
  306.1 0.0 copy-done
  306.2 0.2 select_reduce_fusion
  306.3 0.0 copy-done.1
  306.4 0.2 multiply_reduce_fusion.1
  306.5 0.6 fusion.8
  307.2 0.1 multiply_reduce_fusion
  307.3 0.1 fusion.7
  307.3 0.1 select_n.37
  307.4 9.3 %fusion = bf16[4096,640]{0,1:T(8,128)(2,1)} fusion(bf16[768,4096]{1,0:T(8,128)(2,1)} %reshape.61, f32[768,640]{0,1:T(8,128)S(1)} %get-tuple-element.26, f32[768]{0:T(1024)S(1)} %get-tuple-element.22, f32[768]{0:T(1024)S(1)} %select_n.37, s32[768]{0:T(1024)S(1)} %get-tuple-element.18, s32[640]{0:T(1024)S(1)} %iota_add_fusion, ...), kind=kOutput, calls=%fused_computation.1 | convolution fusion | flops 4033085440 | bytes 13513600 | tf_op jit(solution)/shard_map/dot_general | solution.py:60
  316.7 11.0 %fusion.10 = f32[768,4096]{1,0:T(8,128)} fusion(bf16[4096,640]{1,0:T(8,128)(2,1)} %param.8, f32[768,640]{0,1:T(8,128)S(1)} %get-tuple-element.26, f32[768]{0:T(1024)S(1)} %get-tuple-element.22, f32[768]{0:T(1024)S(1)} %select_n.37, s32[768]{0:T(1024)S(1)} %get-tuple-element.18, s32[640]{0:T(1024)S(1)} %iota_add_fusion, ...), kind=kOutput, calls=%fused_computation.31 | convolution fusion | flops 4030464000 | bytes 19805056 | tf_op jit(solution)/shard_map/dot_general | solution.py:64
  327.7 7.8 %copy.13 = bf16[4096,640]{1,0:T(8,128)(2,1)} copy(bf16[4096,640]{0,1:T(8,128)(2,1)} %fusion) | data formatting | bytes 10485760
  335.5 155.8 %all-reduce.6 = bf16[768,4096]{1,0:T(8,128)(2,1)} all-reduce(f32[768,4096]{1,0:T(8,128)} %fusion.10), channel_id=2, replica_groups=mesh['dp'=16,'vocab'=16] {'dp','vocab'}, use_global_device_ids=true, to_apply=%region_9.10.clone | all-reduce | flops 3145728 | bytes 18874368
  491.3 1.5 dynamic-slice_convert_fusion
  (8 shorter events, 0.0 us)
Async XLA Ops:
  7.2 127.1 %all-gather.3.cloned.1.call-start = ((), (), s32[]{:S(2)}) async-start(), calls=%async_computation | async-start | bytes 8421376 | tf_op jit(solution)/shard_map/all_gather | solution.py:37
  157.1 149.0 %copy-start = (s32[16]{0:T(128)S(1)}, s32[16]{0:T(128)}, u32[]{:S(2)}) copy-start(s32[16]{0:T(128)} %param.11) | copy-start | bytes 196
  157.2 149.2 %copy-start.1 = (f32[16]{0:T(128)S(1)}, f32[16]{0:T(128)}, u32[]{:S(2)}) copy-start(f32[16]{0:T(128)} %param.12) | copy-start | bytes 196
Sparse Core Ops, SparseCore 0:
  11.7 122.4 all-gather.2
where the time goes:
time: 503 us; the launch traced here: 502 us
  blocking collectives  386 us (77%)
  waiting for transfers between devices  41.7 us (8%)
  matrix products  29.5 us (6%)
  local copies, waits for them, and re-layouts  26.4 us (5%)
  between operations  15.9 us (3%)
    unnamed x2, blocking collectives  238 us
    pmax x1, blocking collectives, local(): row_peak = lax.pmax(jnp.max(masked, axis=1), ('dp', 'vocab'))  74.5 us
    psum x1, blocking collectives, local(): lax.psum((local_total, target_part), ('dp', 'vocab'))  73.7 us
    all_gather x1, waiting for transfers between devices, local(): lax.all_gather(hidden, ('dp', 'vocab'), axis=0, tiled=True)  41 us
    unnamed x10, local copies, waits for them, and re-layouts  23.2 us
    dot_general x1, matrix products, local(): lax.dot_general(logit_grad, head_weight, (((1,), (1,)), ((), ())), prefer...  11 us
  transfers between devices with their start and end apart: 1, of which 1 were waited for; matrix products, arithmetic and copies ran while one was open for 1% of the time, Pallas kernels for 0%

commit v1 on v0

v1 whole, which is shorter than its diff:
```python
import functools

import jax
import jax.numpy as jnp
from jax import lax
from jax.experimental import pallas as pl
from jax.experimental.pallas import tpu as pltpu
from jax.sharding import Mesh, PartitionSpec as P

V = 163840
CODES = 32768
WIN = 48
NEG = -1e30
BETA = 1.0
LOSS_SCALE = 4096.0

D = 4096
HALF = D // 2
COLS = 640
TOKENS = 768
META = 128
WIDE = HALF + META
NY, NX, NZ, NC = 4, 4, 8, 2
AXES = ("y", "x", "z", "c")
OFF = (0, 1, 3, 2)
bf16 = jnp.bfloat16
f32 = jnp.float32
VMEM = pl.BlockSpec(memory_space=pltpu.VMEM)
SMEM = pl.BlockSpec(memory_space=pltpu.SMEM)
MB = 1024 * 1024


def flat(y, x, z, c):
    return ((y % NY * NX + x % NX) * NZ + z % NZ) * NC + c


def fetch(value, source):
    pairs = [
        (flat(*source(y, x, z, c)), flat(y, x, z, c))
        for y in range(NY) for x in range(NX) for z in range(NZ) for c in range(NC)
    ]
    return lax.ppermute(value, AXES, pairs)


def middle(step):
    return lambda y, x, z, c: (y + step, x, z, c) if c == 0 else (y, x + step, z, c)


def final(step):
    return lambda y, x, z, c: (y, x + step, z, c) if c == 0 else (y + step, x, z, c)


def along_z(step):
    return lambda y, x, z, c: (y, x, z + step, c)


def along_y(step):
    return lambda y, x, z, c: (y + step, x, z, c)


def along_x(step):
    return lambda y, x, z, c: (y, x + step, z, c)


def near(q):
    return lambda y, x, z, c: (y, x, z ^ (q >> 1), c ^ (q & 1))


def window(ids, core, s, k):
    y, x = ids[0], ids[1]
    across = core == 0
    last = (jnp.where(across, x, y) + OFF[s]) % 4
    mid = (jnp.where(across, y, x) + OFF[k]) % 4
    return jnp.where(across, mid * NX + last, last * NX + mid)


def place(ids, s, q):
    zz, low = ids[2] // 2, ids[2] % 2 * 2 + ids[3]
    return (zz + OFF[s]) % 4 * 4 + (low ^ q)


def call(kernel, outs, ins, scratch=(), vmem=48, **cost):
    return pl.pallas_call(
        kernel,
        out_shape=outs,
        in_specs=ins,
        out_specs=jax.tree.map(lambda _: VMEM, outs),
        scratch_shapes=list(scratch),
        compiler_params=pltpu.CompilerParams(vmem_limit_bytes=vmem * MB),
        cost_estimate=pl.CostEstimate(
            flops=cost.get("flops", 0), bytes_accessed=cost.get("bytes_accessed", 0), transcendentals=0
        ),
    )


def shape(dims, dtype):
    return jax.ShapeDtypeStruct(dims, dtype)


def join_window_kernel(ids, u0, u1, u2, u3, out, tok, meta):
    for s, u in enumerate((u0, u1, u2, u3)):
        for q in range(4):
            dev = place(ids, s, q)
            tok[pl.ds(pl.multiple_of(dev * 48, 16), 48), :] = u[q, 0:48, :].astype(f32)
            meta[pl.ds(pl.multiple_of(dev * 16, 16), 16), :] = u[q, 48:64, :].astype(f32)
    for j in range(3):
        for r in range(16):
            out[j * 16:(j + 1) * 16, r * 128:(r + 1) * 128] = tok[pl.ds(j * 16 + r, 16, stride=48), :].astype(bf16)
        out[j * 16:(j + 1) * 16, HALF:WIDE] = meta[pl.ds(j, 16, stride=16), :].astype(bf16)


def join_window(ids, parts):
    return call(
        join_window_kernel,
        shape((WIN, WIDE), bf16),
        [SMEM] + [VMEM] * 4,
        [pltpu.VMEM((768, 128), f32), pltpu.VMEM((256, 128), f32)],
    )(ids, *parts)


def columns_of(rows):
    full = jnp.concatenate([rows, jnp.zeros((128 - rows.shape[0], 128), f32)], axis=0)
    return full.T


def logits_kernel(ids, a0, a1, a2, a3, b0, b1, b2, b3, head, hidden, logits, stats, target, meta, cols):
    core = ids[3]
    own = pl.multiple_of(core * HALF, HALF)
    oth = pl.multiple_of((1 - core) * HALF, HALF)
    for s, (a, b) in enumerate(((a0, b0), (a1, b1), (a2, b2), (a3, b3))):
        for k in range(4):
            row = pl.multiple_of(window(ids, core, s, k) * WIN, 16)
            hidden[pl.ds(row, WIN), pl.ds(own, HALF)] = a[k, :, 0:HALF]
            meta[pl.ds(row, WIN), :] = a[k, :, HALF:WIDE].astype(f32)
            row = pl.multiple_of(window(ids, 1 - core, s, k) * WIN, 16)
            hidden[pl.ds(row, WIN), pl.ds(oth, HALF)] = b[k, :, 0:HALF]
    first = ids[4] * COLS
    rows = 256
    column = first + lax.broadcasted_iota(jnp.int32, (rows, COLS), 1)
    lane = lax.broadcasted_iota(jnp.int32, (rows, 128), 1)
    for i in range(TOKENS // rows):
        at = pl.ds(i * rows, rows)
        part = jnp.dot(hidden[at, :], head[...], preferred_element_type=f32)
        logits[at, :] = part
        digits = meta[at, :]
        goal = (digits[:, 0:1] + 256.0 * digits[:, 1:2] + 65536.0 * digits[:, 2:3]).astype(jnp.int32)
        in_range = (goal >= V - CODES) == (column >= V - CODES)
        masked = jnp.where(in_range, part, NEG)
        peak = jnp.max(masked, axis=1, keepdims=True)
        total = jnp.sum(jnp.where(in_range, jnp.exp(masked - peak), 0.0), axis=1, keepdims=True)
        hit = jnp.sum(jnp.where(column == goal, part, 0.0), axis=1, keepdims=True)
        cols[at, :] = jnp.where(
            lane == 0, peak, jnp.where(lane == 1, total, jnp.where(lane == 2, hit, goal.astype(f32)))
        )
    stats[...] = jnp.zeros_like(stats)
    target[...] = jnp.zeros_like(target)
    for b in range(TOKENS // 128):
        turned = cols[b * 128:(b + 1) * 128, :].T
        for i in range(3):
            stats[i, b:b + 1, :] = turned[i:i + 1, :]
        target[b:b + 1, :] = turned[3:4, :]


def local_logits(ids, own, other, head):
    return call(
        logits_kernel,
        (
            shape((TOKENS, D), bf16),
            shape((TOKENS, COLS), f32),
            shape((3, 8, 128), f32),
            shape((8, 128), f32),
        ),
        [SMEM] + [VMEM] * 9,
        [pltpu.VMEM((TOKENS, 128), f32), pltpu.VMEM((TOKENS, 128), f32)],
        flops=2 * TOKENS * D * COLS,
        bytes_accessed=25 * MB,
    )(ids, *own, *other, head)


def merge_kernel(a, b, c, d, out):
    peak = jnp.maximum(jnp.maximum(a[0], b[0]), jnp.maximum(c[0], d[0]))
    term = [v[1] * jnp.exp(v[0] - peak) for v in (a, b, c, d)]
    out[0] = peak
    out[1] = (term[0] + term[1]) + (term[2] + term[3])
    out[2] = (a[2] + b[2]) + (c[2] + d[2])


def merge(a, b, c, d):
    return call(merge_kernel, shape((3, 8, 128), f32), [VMEM] * 4)(a, b, c, d)


def preference(stats, lengths, ref_logps, pairing):
    rows = lax.broadcasted_iota(jnp.int32, (1, TOKENS), 1)
    inner = rows % WIN
    position = inner % 16 * 3 + inner // 16
    log_norm = stats[0] + jnp.log(jnp.maximum(stats[1], 1e-37))
    token_lp = (stats[2] - log_norm)[:6].reshape(1, TOKENS)
    groups = lengths.shape[0]
    members = jnp.arange(groups, dtype=jnp.int32)
    is_valid = (rows // WIN == members[:, None]) & (position < lengths[:, None])
    token_count = lengths.astype(f32)
    policy = jnp.sum(jnp.where(is_valid, token_lp, 0.0), axis=1) / token_count
    shifted = policy - ref_logps
    chosen = (pairing[0::2][:, None] == members[None, :]).astype(f32)
    rejected = (pairing[1::2][:, None] == members[None, :]).astype(f32)
    pair_signs = chosen - rejected
    margin = BETA * jnp.sum(pair_signs * shifted[None, :], axis=1)
    mean_loss = jnp.mean(jax.nn.softplus(-margin))
    pair_weight = -LOSS_SCALE * BETA * jax.nn.sigmoid(-margin) / margin.shape[0]
    group_weight = jnp.sum(pair_weight[:, None] * pair_signs, axis=0) / token_count
    token_weight = jnp.sum(jnp.where(is_valid, group_weight[:, None], 0.0), axis=0)
    weight = jnp.pad(token_weight.reshape(6, 128), ((0, 2), (0, 0)))
    return mean_loss, log_norm, weight


BLOCK = 512


def grad_kernel(ids, logits, norm, weight, target, head, grad, out):
    @pl.when(pl.program_id(0) == 0)
    def _():
        norm_c, weight_c, goal_c = columns_of(norm[...]), columns_of(weight[...]), columns_of(target[...])
        column = ids[4] * COLS + lax.broadcasted_iota(jnp.int32, (128, COLS), 1)
        for b in range(TOKENS // 128):
            goal = goal_c[:, b:b + 1].astype(jnp.int32)
            in_range = (goal >= V - CODES) == (column >= V - CODES)
            at = slice(b * 128, (b + 1) * 128)
            prob = jnp.exp(jnp.where(in_range, logits[at, :] - norm_c[:, b:b + 1], NEG))
            grad[at, :] = (weight_c[:, b:b + 1] * ((column == goal).astype(f32) - prob)).astype(bf16)

    out[...] = lax.dot_general(
        grad[...], head[...], (((1,), (1,)), ((), ())), preferred_element_type=f32
    ).astype(out.dtype)


def grad_other(ids, logits, norm, weight, target, head):
    return pl.pallas_call(
        grad_kernel,
        grid_spec=pltpu.PrefetchScalarGridSpec(
            num_scalar_prefetch=1,
            grid=(HALF // BLOCK,),
            in_specs=[
                pl.BlockSpec((TOKENS, COLS), lambda i, ids: (0, 0)),
                pl.BlockSpec((8, 128), lambda i, ids: (0, 0)),
                pl.BlockSpec((8, 128), lambda i, ids: (0, 0)),
                pl.BlockSpec((8, 128), lambda i, ids: (0, 0)),
                pl.BlockSpec((BLOCK, COLS), lambda i, ids: ((1 - ids[3]) * (HALF // BLOCK) + i, 0)),
            ],
            out_specs=[
                pl.BlockSpec((TOKENS, COLS), lambda i, ids: (0, 0)),
                pl.BlockSpec((TOKENS, BLOCK), lambda i, ids: (0, i)),
            ],
        ),
        out_shape=(shape((TOKENS, COLS), bf16), shape((TOKENS, HALF), bf16)),
        compiler_params=pltpu.CompilerParams(vmem_limit_bytes=40 * MB),
        cost_estimate=pl.CostEstimate(flops=TOKENS * D * COLS, bytes_accessed=9 * MB, transcendentals=0),
    )(ids, logits, norm, weight, target, head)


def grad_own_kernel(ids, grad, head, out):
    out[...] = lax.dot_general(
        grad[...], head[...], (((1,), (1,)), ((), ())), preferred_element_type=f32
    ).astype(out.dtype)


def grad_own(ids, grad, head):
    return pl.pallas_call(
        grad_own_kernel,
        grid_spec=pltpu.PrefetchScalarGridSpec(
            num_scalar_prefetch=1,
            grid=(HALF // BLOCK,),
            in_specs=[
                pl.BlockSpec((TOKENS, COLS), lambda i, ids: (0, 0)),
                pl.BlockSpec((BLOCK, COLS), lambda i, ids: (ids[3] * (HALF // BLOCK) + i, 0)),
            ],
            out_specs=pl.BlockSpec((TOKENS, BLOCK), lambda i, ids: (0, i)),
        ),
        out_shape=shape((TOKENS, HALF), f32),
        compiler_params=pltpu.CompilerParams(vmem_limit_bytes=40 * MB),
        cost_estimate=pl.CostEstimate(flops=TOKENS * D * COLS, bytes_accessed=10 * MB, transcendentals=0),
    )(ids, grad, head)


def head_kernel(hidden, grad, out):
    out[...] = lax.dot_general(
        hidden[...], grad[...], (((0,), (0,)), ((), ())), preferred_element_type=f32
    ).astype(out.dtype)


def grad_head_of(hidden, grad):
    return pl.pallas_call(
        head_kernel,
        grid=(D // BLOCK,),
        in_specs=[
            pl.BlockSpec((TOKENS, BLOCK), lambda i: (0, i)),
            pl.BlockSpec((TOKENS, COLS), lambda i: (0, 0)),
        ],
        out_specs=pl.BlockSpec((BLOCK, COLS), lambda i: (i, 0)),
        out_shape=shape((D, COLS), bf16),
        compiler_params=pltpu.CompilerParams(vmem_limit_bytes=40 * MB),
        cost_estimate=pl.CostEstimate(flops=2 * TOKENS * D * COLS, bytes_accessed=12 * MB, transcendentals=0),
    )(hidden, grad)


def split_final_kernel(order, own, other, r0, r1, r2, r3):
    total = own[...] + other[...].astype(f32)
    step = pl.program_id(0)
    for s, r in enumerate((r0, r1, r2, r3)):
        @pl.when(step // 4 == s)
        def _(r=r):
            r[0] = total.astype(r.dtype)


def split_final(order, own, other):
    block = pl.BlockSpec((WIN, HALF), lambda i, order: (order[i], 0))

    def out(s):
        return pl.BlockSpec((1, WIN, HALF), lambda i, order: (jnp.clip(i - 4 * s, 0, 3), 0, 0))

    return pl.pallas_call(
        split_final_kernel,
        grid_spec=pltpu.PrefetchScalarGridSpec(
            num_scalar_prefetch=1,
            grid=(16,),
            in_specs=[block, block],
            out_specs=[out(s) for s in range(4)],
        ),
        out_shape=[shape((4, WIN, HALF), f32 if s == 0 else bf16) for s in range(4)],
        cost_estimate=pl.CostEstimate(flops=0, bytes_accessed=14 * MB, transcendentals=0),
    )(order, own, other)


def add_four(a, b, c, d):
    return (a.astype(f32) + d.astype(f32)) + (b.astype(f32) + c.astype(f32))


def split_middle_kernel(a, b, c, d, q0, q1, q2, q3):
    for k, q in enumerate((q0, q1, q2, q3)):
        q[...] = add_four(a[k], b[k], c[k], d[k]).astype(q.dtype)


def split_middle(a, b, c, d):
    return call(
        split_middle_kernel,
        [shape((WIN, HALF), f32 if k == 0 else bf16) for k in range(4)],
        [VMEM] * 4,
        bytes_accessed=6 * MB,
    )(a, b, c, d)


def split_window_kernel(ids, a, b, c, d, u0, u1, u2, u3, tok):
    total = add_four(a[...], b[...], c[...], d[...])
    for j in range(3):
        for r in range(16):
            tok[pl.ds(j * 16 + r, 16, stride=48), :] = total[j * 16:(j + 1) * 16, r * 128:(r + 1) * 128]
    for s, u in enumerate((u0, u1, u2, u3)):
        for q in range(4):
            dev = place(ids, s, q)
            u[q] = tok[pl.ds(pl.multiple_of(dev * 48, 16), 48), :].astype(u.dtype)


def split_window(ids, a, b, c, d):
    return call(
        split_window_kernel,
        [shape((4, 48, 128), f32 if s == 0 else bf16) for s in range(4)],
        [SMEM] + [VMEM] * 4,
        [pltpu.VMEM((768, 128), f32)],
    )(ids, a, b, c, d)


def split_near_kernel(a, b, c, d, v0, v1, v2, v3):
    for q, v in enumerate((v0, v1, v2, v3)):
        v[...] = add_four(a[q], b[q], c[q], d[q]).astype(v.dtype)


def split_near(a, b, c, d):
    return call(
        split_near_kernel,
        [shape((48, 128), f32 if q == 0 else bf16) for q in range(4)],
        [VMEM] * 4,
    )(a, b, c, d)


def local(hidden, head_weight, targets, image_mask, lengths, ref_logps, pairing):
    y, x, z, c = (lax.axis_index(a) for a in AXES)
    ids = jnp.stack([y, x, z, c, flat(y, x, z, c)]).astype(jnp.int32)

    digits = jnp.stack([targets % 256, targets // 256 % 256, targets // 65536], axis=1)
    meta = jnp.pad(digits.astype(f32).astype(bf16), ((0, 13), (0, 125)))
    halves = hidden.reshape(3, 2, 16, 128)
    first, second = (jnp.concatenate([halves[:, i].reshape(48, 128), meta], axis=0) for i in range(2))
    mine = jnp.where(c == 0, first, second)
    theirs = jnp.where(c == 0, second, first)

    near_parts = jnp.stack(
        [mine, fetch(theirs, near(1)), fetch(mine, near(2)), fetch(theirs, near(3))]
    )
    z_parts = [near_parts] + [fetch(near_parts, along_z(2 * o)) for o in OFF[1:]]
    block = join_window(ids, z_parts)
    blocks = jnp.stack([block] + [fetch(block, middle(o)) for o in OFF[1:]])
    own = [blocks] + [fetch(blocks, final(o)) for o in OFF[1:]]
    other = [fetch(v, near(1)) for v in own]

    rows, logits, stats, target = local_logits(ids, own, other, head_weight)
    stats = merge(stats, *(fetch(stats, near(q)) for q in (1, 2, 3)))
    for ring in (lambda o: along_z(2 * o), along_y, along_x):
        stats = merge(stats, *(fetch(stats, ring(o)) for o in (2, 1, 3)))
    mean_loss, log_norm, weight = preference(stats, lengths, ref_logps, pairing)

    logit_grad, send = grad_other(ids, logits, log_norm, weight, target, head_weight)
    received = fetch(send, near(1))
    keep = grad_own(ids, logit_grad, head_weight)
    grad_head = grad_head_of(rows, logit_grad)

    order = jnp.stack([window(ids, c, s, k) for s in range(4) for k in range(4)]).astype(jnp.int32)
    parts = split_final(order, keep, received)
    parts = split_middle(parts[0], *(fetch(parts[s], final(-OFF[s])) for s in (1, 2, 3)))
    parts = split_window(ids, parts[0], *(fetch(parts[s], middle(-OFF[s])) for s in (1, 2, 3)))
    parts = split_near(parts[0], *(fetch(parts[s], along_z(-2 * OFF[s])) for s in (1, 2, 3)))
    far1, near2, far3 = (fetch(parts[q], near(q)) for q in (1, 2, 3))
    own_half = (parts[0] + near2.astype(f32)).astype(bf16).reshape(3, HALF)
    other_half = (far1.astype(f32) + far3.astype(f32)).astype(bf16).reshape(3, HALF)
    grad_hidden = jnp.where(
        c == 0,
        jnp.concatenate([own_half, other_half], axis=1),
        jnp.concatenate([other_half, own_half], axis=1),
    )
    return grad_hidden, grad_head, mean_loss


def solution(mesh):
    fine = Mesh(mesh.devices.reshape(NY, NX, NZ, NC), AXES)
    return jax.shard_map(
        local,
        mesh=fine,
        in_specs=(P(AXES, None), P(None, AXES), P(AXES), P(AXES), P(), P(), P()),
        out_specs=(P(AXES, None), P(None, AXES), P()),
        check_vma=False,
    )
```

time: 503 us -> 225 us (0.45)
  blocking collectives: 386 us -> 0 us
  starting transfers between devices: 0.04 us -> 104 us
  Pallas kernels: 0 us -> 42.2 us
  matrix products: 29.5 us -> 0 us
  between operations: 15.9 us -> 2.75 us
  waiting for transfers between devices: 41.7 us -> 54.7 us
  local copies, waits for them, and re-layouts: 26.4 us -> 15.4 us
    unnamed x2 -> x0, blocking collectives: 238 us -> none
    ppermute x0 -> x41, starting transfers between devices: none -> 104 us  [fetch(): return lax.ppermute(value, AXES, pairs)]
    pmax x1 -> x0, blocking collectives: 74.5 us -> none  [local(): row_peak = lax.pmax(jnp.max(masked, axis=1), ('dp', 'vocab'))]
    psum x1 -> x0, blocking collectives: 73.7 us -> none  [local(): lax.psum((local_total, target_part), ('dp', 'vocab'))]
    ppermute x0 -> x41, waiting for transfers between devices: none -> 54.7 us  [fetch(): return lax.ppermute(value, AXES, pairs)]
    pallas_call x0 -> x13, Pallas kernels: none -> 42.2 us  [the longest x1 12.4 us: split_final(): pl.pallas_call(split_final_kernel, grid_spec=pltpu.PrefetchScalarGridSpec...]
    all_gather x1 -> x0, waiting for transfers between devices: 41 us -> none  [local(): lax.all_gather(hidden, ('dp', 'vocab'), axis=0, tiled=True)]
    dot_general x3 -> x0, matrix products: 29.5 us -> none  [the longest x1 11 us: local(): lax.dot_general(logit_grad, head_weight, (((1,), (1,)), ((), ())), prefer...]
  transfers between devices with their start and end apart: 1 -> 41, of which waited for: 1 -> 22; matrix products, arithmetic and copies ran while one was open for 1% -> 0% of each run, Pallas kernels for 0% -> 5%
where the time goes in v1:
time: 225 us; the launch traced here: 222 us
  starting transfers between devices  104 us (46%)
  waiting for transfers between devices  54.7 us (24%)
  Pallas kernels  42.2 us (19%)
  local copies, waits for them, and re-layouts  15.4 us (7%)
  other arithmetic  2.75 us (1%)
  between operations  2.75 us (1%)
    ppermute x41, starting transfers between devices, fetch(): return lax.ppermute(value, AXES, pairs)  104 us
    ppermute x41, waiting for transfers between devices, fetch(): return lax.ppermute(value, AXES, pairs)  54.7 us
    unnamed x21, local copies, waits for them, and re-layouts  14.2 us
    pallas_call x1, Pallas kernels, split_final(): pl.pallas_call(split_final_kernel, grid_spec=pltpu.PrefetchScalarGridSpec...  12.4 us
    pallas_call x1, Pallas kernels, local_logits(): call(logits_kernel, (shape((TOKENS, D), bf16), shape((TOKENS, COLS), f32)...  10.1 us
    pallas_call x1, Pallas kernels, grad_head_of(): pl.pallas_call(head_kernel, grid=(D // BLOCK,), in_specs=[pl.BlockSpec((T...  7.92 us
    pallas_call x1, Pallas kernels, grad_other(): pl.pallas_call(grad_kernel, grid_spec=pltpu.PrefetchScalarGridSpec(num_sc...  5.68 us
  transfers between devices with their start and end apart: 41, of which 22 were waited for; matrix products, arithmetic and copies ran while one was open for 0% of the time, Pallas kernels for 5%

profile of v1, /device:TPU:1, one launch (start us, length us, event | category | flops | bytes accessed | tf_op | source)
XLA Modules:
  0.0 221.8 jit_solution(5216372902406729098)
XLA Ops:
  2.5 3.1 %collective-permute-start.2 = (bf16[64,128]{1,0:T(8,128)(2,1)S(1)}, bf16[64,128]{1,0:T(8,128)(2,1)S(1)}, u32[]{:S(2)}, u32[]{:S(2)}) collective-permute-start(bf16[64,128]{1,0:T(8,128)(2,1)S(1)} %get-tuple-element.50), channel_id=1, source_target_pairs={{3,0},{2,1},{1,2},{0,3},{7,4},{6,5},{5,6},{4,7},{11,8},{10,9},{9,1... | collective-permute-start | bytes 49160 | tf_op jit(solution)/shard_map/ppermute | solution.py:42
  8.6 5.7 %collective-permute-start.5 = (bf16[4,64,128]{2,1,0:T(8,128)(2,1)S(1)}, bf16[4,64,128]{2,1,0:T(8,128)(2,1)S(1)}, u32[]{:S(2)}, u32[]{:S(2)}) collective-permute-start(bf16[4,64,128]{2,1,0:T(8,128)(2,1)S(1)} %pad_maximum_fusion.1.u0), channel_id=1, source_target_pairs={{8,0},{9,1},{10,2},{11,3},{12,4},{13,5},{14,6},{15,7},{0,8},{1,9},... | collective-permute-start | bytes 196616 | tf_op jit(solution)/shard_map/ppermute | solution.py:42
  15.5 2.4 %collective-permute-start.3 = (bf16[4,64,128]{2,1,0:T(8,128)(2,1)S(1)}, bf16[4,64,128]{2,1,0:T(8,128)(2,1)S(1)}, u32[]{:S(2)}, u32[]{:S(2)}) collective-permute-start(bf16[4,64,128]{2,1,0:T(8,128)(2,1)S(1)} %pad_maximum_fusion.1.u0), channel_id=1, source_target_pairs={{4,0},{5,1},{6,2},{7,3},{8,4},{9,5},{10,6},{11,7},{12,8},{13,9},{1... | collective-permute-start | bytes 196616 | tf_op jit(solution)/shard_map/ppermute | solution.py:42
  21.2 2.8 %collective-permute-start.8 = (bf16[48,2176]{1,0:T(8,128)(2,1)S(1)}, bf16[48,2176]{1,0:T(8,128)(2,1)S(1)}, u32[]{:S(2)}, u32[]{:S(2)}) collective-permute-start(bf16[48,2176]{1,0:T(8,128)(2,1)S(1)} %shard_map.85), channel_id=1, source_target_pairs={{128,0},{33,1},{130,2},{35,3},{132,4},{37,5},{134,6},{39,7},{136,8... | collective-permute-start | bytes 626696 | tf_op jit(solution)/shard_map/ppermute | solution.py:42
  27.5 2.7 %collective-permute-done.7 = bf16[48,2176]{1,0:T(8,128)(2,1)S(1)} collective-permute-done((bf16[48,2176]{1,0:T(8,128)(2,1)S(1)}, bf16[48,2176]{1,0:T(8,128)(2,1)S(1)}, u32[]{:S(2)}, u32[]{:S(2)}) %collective-permute-start.7) | collective-permute-done | bytes 208928 | tf_op jit(solution)/shard_map/ppermute | solution.py:42
  30.4 2.9 %collective-permute-start.11 = (bf16[4,48,2176]{2,1,0:T(8,128)(2,1)S(1)}, bf16[4,48,2176]{2,1,0:T(8,128)(2,1)S(1)}, u32[]{:S(2)}, u32[]{:S(2)}) collective-permute-start(bf16[4,48,2176]{2,1,0:T(8,128)(2,1)S(1)} %pad_maximum_fusion.a0), channel_id=1, source_target_pairs={{32,0},{129,1},{34,2},{131,3},{36,4},{133,5},{38,6},{135,7},{40,8}... | collective-permute-start | bytes 2506760 | tf_op jit(solution)/shard_map/ppermute | solution.py:42
  35.9 14.0 %collective-permute-start.12 = (bf16[4,48,2176]{2,1,0:T(8,128)(2,1)S(1)}, bf16[4,48,2176]{2,1,0:T(8,128)(2,1)S(1)}, u32[]{:S(2)}, u32[]{:S(2)}) collective-permute-start(bf16[4,48,2176]{2,1,0:T(8,128)(2,1)S(1)} %pad_maximum_fusion.a0), channel_id=1, source_target_pairs={{1,0},{0,1},{3,2},{2,3},{5,4},{4,5},{7,6},{6,7},{9,8},{8,9},{11,10... | collective-permute-start | bytes 2506760 | tf_op jit(solution)/shard_map/ppermute | solution.py:42
  49.9 7.4 %collective-permute-start.15 = (bf16[4,48,2176]{2,1,0:T(8,128)(2,1)S(1)}, bf16[4,48,2176]{2,1,0:T(8,128)(2,1)S(1)}, u32[]{:S(2)}, u32[]{:S(2)}) collective-permute-start(bf16[4,48,2176]{2,1,0:T(8,128)(2,1)S(1)} %collective-permute-done.11.a3), channel_id=1, source_target_pairs={{1,0},{0,1},{3,2},{2,3},{5,4},{4,5},{7,6},{6,7},{9,8},{8,9},{11,10... | collective-permute-start | bytes 2506760 | tf_op jit(solution)/shard_map/ppermute | solution.py:42
  57.3 8.8 %collective-permute-start.14 = (bf16[4,48,2176]{2,1,0:T(8,128)(2,1)S(1)}, bf16[4,48,2176]{2,1,0:T(8,128)(2,1)S(1)}, u32[]{:S(2)}, u32[]{:S(2)}) collective-permute-start(bf16[4,48,2176]{2,1,0:T(8,128)(2,1)S(1)} %collective-permute-done.10.a2), channel_id=1, source_target_pairs={{1,0},{0,1},{3,2},{2,3},{5,4},{4,5},{7,6},{6,7},{9,8},{8,9},{11,10... | collective-permute-start | bytes 2506760 | tf_op jit(solution)/shard_map/ppermute | solution.py:42
  69.3 10.1 %shard_map.86 = (bf16[768,4096]{1,0:T(8,128)(2,1)}, f32[768,640]{1,0:T(8,128)}, f32[3,8,128]{2,1,0:T(8,128)S(1)}, f32[8,128]{1,0:T(8,128)S(1)}) custom-call(s32[5]{0:T(128)S(1)} %stack.114.ids, bf16[4,48,2176]{2,1,0:T(8,128)(2,1)S(1)} %pad_maximum_fusion.a0, bf16[4,48,2176]{2,1,0:T(8,128)(2,1)S(1)} %collective-permute-done.9.a1, ...), custom_call_target="tpu_custom_call" | custom-call | flops 4026531840 | bytes 26214400 | tf_op jit(solution)/shard_map/pallas_call | solution.py:165
  83.5 3.6 %collective-permute-start.20 = (f32[3,8,128]{2,1,0:T(8,128)S(1)}, f32[3,8,128]{2,1,0:T(8,128)S(1)}, u32[]{:S(2)}, u32[]{:S(2)}) collective-permute-start(f32[3,8,128]{2,1,0:T(8,128)S(1)} %shard_map.87.a), channel_id=1, source_target_pairs={{4,0},{5,1},{6,2},{7,3},{8,4},{9,5},{10,6},{11,7},{12,8},{13,9},{1... | collective-permute-start | bytes 36872 | tf_op jit(solution)/shard_map/ppermute | solution.py:42
  88.9 4.5 %collective-permute-done.19.b = f32[3,8,128]{2,1,0:T(8,128)S(1)} collective-permute-done((f32[3,8,128]{2,1,0:T(8,128)S(1)}, f32[3,8,128]{2,1,0:T(8,128)S(1)}, u32[]{:S(2)}, u32[]{:S(2)}) %collective-permute-start.19) | collective-permute-done | bytes 12320 | tf_op jit(solution)/shard_map/ppermute | solution.py:42
  93.9 3.0 %collective-permute-start.23 = (f32[3,8,128]{2,1,0:T(8,128)S(1)}, f32[3,8,128]{2,1,0:T(8,128)S(1)}, u32[]{:S(2)}, u32[]{:S(2)}) collective-permute-start(f32[3,8,128]{2,1,0:T(8,128)S(1)} %shard_map.88.a), channel_id=1, source_target_pairs={{64,0},{65,1},{66,2},{67,3},{68,4},{69,5},{70,6},{71,7},{72,8},{73... | collective-permute-start | bytes 36872 | tf_op jit(solution)/shard_map/ppermute | solution.py:42
  97.9 2.9 %collective-permute-done.22.b = f32[3,8,128]{2,1,0:T(8,128)S(1)} collective-permute-done((f32[3,8,128]{2,1,0:T(8,128)S(1)}, f32[3,8,128]{2,1,0:T(8,128)S(1)}, u32[]{:S(2)}, u32[]{:S(2)}) %collective-permute-start.22) | collective-permute-done | bytes 12320 | tf_op jit(solution)/shard_map/ppermute | solution.py:42
  100.9 11.6 %collective-permute-start.27 = (f32[3,8,128]{2,1,0:T(8,128)S(1)}, f32[3,8,128]{2,1,0:T(8,128)S(1)}, u32[]{:S(2)}, u32[]{:S(2)}) collective-permute-start(f32[3,8,128]{2,1,0:T(8,128)S(1)} %shard_map.89.a), channel_id=1, source_target_pairs={{48,0},{49,1},{50,2},{51,3},{52,4},{53,5},{54,6},{55,7},{56,8},{57... | collective-permute-start | bytes 36872 | tf_op jit(solution)/shard_map/ppermute | solution.py:42
  115.0 2.4 %collective-permute-done.25.b = f32[3,8,128]{2,1,0:T(8,128)S(1)} collective-permute-done((f32[3,8,128]{2,1,0:T(8,128)S(1)}, f32[3,8,128]{2,1,0:T(8,128)S(1)}, u32[]{:S(2)}, u32[]{:S(2)}) %collective-permute-start.25) | collective-permute-done | bytes 12320 | tf_op jit(solution)/shard_map/ppermute | solution.py:42
  118.7 2.5 %copy-done.1 = bf16[4096,640]{1,0:T(8,128)(2,1)S(1)} copy-done((bf16[4096,640]{1,0:T(8,128)(2,1)S(1)}, bf16[4096,640]{1,0:T(8,128)(2,1)}, u32[]{:S(2)}) %copy-start.1) | copy-done | bytes 5242904
  122.7 5.7 %shard_map.91 = (bf16[768,640]{1,0:T(8,128)(2,1)S(1)}, bf16[768,2048]{1,0:T(8,128)(2,1)}) custom-call(s32[5]{0:T(128)S(1)} %stack.114.ids, f32[768,640]{1,0:T(8,128)S(1)} %copy-done.4, f32[8,128]{1,0:T(8,128)S(1)} %get-tuple-element.48.norm, f32[8,128]{1,0:T(8,128)S(1)} %pad.9.weight, f32[8,128]{1,0:T(8,128)S(1)} %get-tuple-element.27.target, ...), custom_call_target="tpu_custom_call" | custom-call | flops 2013265920 | bytes 9437184 | tf_op jit(solution)/shard_map/pallas_call | solution.py:237
  128.4 6.1 %collective-permute-start.28 = (bf16[768,2048]{1,0:T(8,128)(2,1)}, bf16[768,2048]{1,0:T(8,128)(2,1)}, u32[]{:S(2)}, u32[]{:S(2)}) collective-permute-start(bf16[768,2048]{1,0:T(8,128)(2,1)} %get-tuple-element.29), channel_id=1, source_target_pairs={{1,0},{0,1},{3,2},{2,3},{5,4},{4,5},{7,6},{6,7},{9,8},{8,9},{11,10... | collective-permute-start | bytes 9437192 | tf_op jit(solution)/shard_map/ppermute | solution.py:42
  135.2 2.5 %copy-done.2 = bf16[4096,640]{1,0:T(8,128)(2,1)S(1)} copy-done((bf16[4096,640]{1,0:T(8,128)(2,1)S(1)}, bf16[4096,640]{1,0:T(8,128)(2,1)}, u32[]{:S(2)}) %copy-start.2) | copy-done | bytes 5242904
  137.6 4.2 %shard_map.92.own = f32[768,2048]{1,0:T(8,128)S(1)} custom-call(s32[5]{0:T(128)S(1)} %stack.114.ids, bf16[768,640]{1,0:T(8,128)(2,1)S(1)} %get-tuple-element.28.grad, bf16[4096,640]{1,0:T(8,128)(2,1)S(1)} %copy-done.2), custom_call_target="tpu_custom_call" | custom-call | flops 2013265920 | bytes 10485760 | tf_op jit(solution)/shard_map/pallas_call | solution.py:267
  141.9 2.7 %copy-done = f32[768,2048]{1,0:T(8,128)} copy-done((f32[768,2048]{1,0:T(8,128)}, f32[768,2048]{1,0:T(8,128)S(1)}, u32[]{:S(2)}) %copy-start) | copy-done | bytes 6291480
  144.5 12.4 %shard_map.93 = (f32[4,48,2048]{2,1,0:T(8,128)}, bf16[4,48,2048]{2,1,0:T(8,128)(2,1)}, bf16[4,48,2048]{2,1,0:T(8,128)(2,1)}, bf16[4,48,2048]{2,1,0:T(8,128)(2,1)}) custom-call(s32[16]{0:T(128)} %stack.131.order, f32[768,2048]{1,0:T(8,128)} %copy-done, bf16[768,2048]{1,0:T(8,128)(2,1)} %collective-permute-done.28.other), custom_call_target="tpu_custom_call" | custom-call | bytes 14680064 | tf_op jit(solution)/shard_map/pallas_call | solution.py:320
  156.9 2.7 %collective-permute-start.30 = (bf16[4,48,2048]{2,1,0:T(8,128)(2,1)}, bf16[4,48,2048]{2,1,0:T(8,128)(2,1)S(1)}, u32[]{:S(2)}, u32[]{:S(2)}) collective-permute-start(bf16[4,48,2048]{2,1,0:T(8,128)(2,1)} %get-tuple-element.32), channel_id=1, source_target_pairs={{16,0},{65,1},{18,2},{67,3},{20,4},{69,5},{22,6},{71,7},{24,8},{73... | collective-permute-start | bytes 2359304 | tf_op jit(solution)/shard_map/ppermute | solution.py:42
  159.7 9.7 %collective-permute-done.29.b = bf16[4,48,2048]{2,1,0:T(8,128)(2,1)S(1)} collective-permute-done((bf16[4,48,2048]{2,1,0:T(8,128)(2,1)}, bf16[4,48,2048]{2,1,0:T(8,128)(2,1)S(1)}, u32[]{:S(2)}, u32[]{:S(2)}) %collective-permute-start.29) | collective-permute-done | bytes 786464 | tf_op jit(solution)/shard_map/ppermute | solution.py:42
  169.4 7.8 %collective-permute-done.30.c = bf16[4,48,2048]{2,1,0:T(8,128)(2,1)S(1)} collective-permute-done((bf16[4,48,2048]{2,1,0:T(8,128)(2,1)}, bf16[4,48,2048]{2,1,0:T(8,128)(2,1)S(1)}, u32[]{:S(2)}, u32[]{:S(2)}) %collective-permute-start.30) | collective-permute-done | bytes 786464 | tf_op jit(solution)/shard_map/ppermute | solution.py:42
  182.2 3.3 %collective-permute-done.32.b = bf16[48,2048]{1,0:T(8,128)(2,1)S(1)} collective-permute-done((bf16[48,2048]{1,0:T(8,128)(2,1)S(1)}, bf16[48,2048]{1,0:T(8,128)(2,1)S(1)}, u32[]{:S(2)}, u32[]{:S(2)}) %collective-permute-start.32) | collective-permute-done | bytes 196640 | tf_op jit(solution)/shard_map/ppermute | solution.py:42
  189.4 3.6 %collective-permute-start.36 = (bf16[4,48,128]{2,1,0:T(8,128)(2,1)S(1)}, bf16[4,48,128]{2,1,0:T(8,128)(2,1)S(1)}, u32[]{:S(2)}, u32[]{:S(2)}) collective-permute-start(bf16[4,48,128]{2,1,0:T(8,128)(2,1)S(1)} %get-tuple-element.40), channel_id=1, source_target_pairs={{4,0},{5,1},{6,2},{7,3},{8,4},{9,5},{10,6},{11,7},{12,8},{13,9},{1... | collective-permute-start | bytes 147464 | tf_op jit(solution)/shard_map/ppermute | solution.py:42
  194.6 5.8 %collective-permute-done.37.d = bf16[4,48,128]{2,1,0:T(8,128)(2,1)S(1)} collective-permute-done((bf16[4,48,128]{2,1,0:T(8,128)(2,1)S(1)}, bf16[4,48,128]{2,1,0:T(8,128)(2,1)S(1)}, u32[]{:S(2)}, u32[]{:S(2)}) %collective-permute-start.37) | collective-permute-done | bytes 49184 | tf_op jit(solution)/shard_map/ppermute | solution.py:42
  201.6 2.8 %copy-done.5 = bf16[768,4096]{1,0:T(8,128)(2,1)S(1)} copy-done((bf16[768,4096]{1,0:T(8,128)(2,1)S(1)}, bf16[768,4096]{1,0:T(8,128)(2,1)}, u32[]{:S(2)}) %copy-start.5) | copy-done | bytes 6291480
  204.3 7.9 %shard_map.97 = bf16[4096,640]{1,0:T(8,128)(2,1)} custom-call(bf16[768,4096]{1,0:T(8,128)(2,1)S(1)} %copy-done.5, bf16[768,640]{1,0:T(8,128)(2,1)S(1)} %get-tuple-element.28.grad), custom_call_target="tpu_custom_call" | custom-call | flops 4026531840 | bytes 12582912 | tf_op jit(solution)/shard_map/pallas_call | solution.py:291
  212.8 3.8 %collective-permute-start.39 = (bf16[48,128]{1,0:T(8,128)(2,1)S(1)}, bf16[48,128]{1,0:T(8,128)(2,1)S(1)}, u32[]{:S(2)}, u32[]{:S(2)}) collective-permute-start(bf16[48,128]{1,0:T(8,128)(2,1)S(1)} %get-tuple-element.44), channel_id=1, source_target_pairs={{1,0},{0,1},{3,2},{2,3},{5,4},{4,5},{7,6},{6,7},{9,8},{8,9},{11,10... | collective-permute-start | bytes 36872 | tf_op jit(solution)/shard_map/ppermute | solution.py:42
  (115 shorter events, 47.6 us)
Async XLA Ops:
  2.5 6.1 %collective-permute-start.2 = (bf16[64,128]{1,0:T(8,128)(2,1)S(1)}, bf16[64,128]{1,0:T(8,128)(2,1)S(1)}, u32[]{:S(2)}, u32[]{:S(2)}) collective-permute-start(bf16[64,128]{1,0:T(8,128)(2,1)S(1)} %get-tuple-element.50), channel_id=1, source_target_pairs={{3,0},{2,1},{1,2},{0,3},{7,4},{6,5},{5,6},{4,7},{11,8},{10,9},{9,1... | collective-permute-start | bytes 49160 | tf_op jit(solution)/shard_map/ppermute | solution.py:42
  8.6 9.4 %collective-permute-start.5 = (bf16[4,64,128]{2,1,0:T(8,128)(2,1)S(1)}, bf16[4,64,128]{2,1,0:T(8,128)(2,1)S(1)}, u32[]{:S(2)}, u32[]{:S(2)}) collective-permute-start(bf16[4,64,128]{2,1,0:T(8,128)(2,1)S(1)} %pad_maximum_fusion.1.u0), channel_id=1, source_target_pairs={{8,0},{9,1},{10,2},{11,3},{12,4},{13,5},{14,6},{15,7},{0,8},{1,9},... | collective-permute-start | bytes 196616 | tf_op jit(solution)/shard_map/ppermute | solution.py:42
  14.3 6.0 %collective-permute-start.4 = (bf16[4,64,128]{2,1,0:T(8,128)(2,1)S(1)}, bf16[4,64,128]{2,1,0:T(8,128)(2,1)S(1)}, u32[]{:S(2)}, u32[]{:S(2)}) collective-permute-start(bf16[4,64,128]{2,1,0:T(8,128)(2,1)S(1)} %pad_maximum_fusion.1.u0), channel_id=1, source_target_pairs={{12,0},{13,1},{14,2},{15,3},{0,4},{1,5},{2,6},{3,7},{4,8},{5,9},{6... | collective-permute-start | bytes 196616 | tf_op jit(solution)/shard_map/ppermute | solution.py:42
  15.5 5.0 %collective-permute-start.3 = (bf16[4,64,128]{2,1,0:T(8,128)(2,1)S(1)}, bf16[4,64,128]{2,1,0:T(8,128)(2,1)S(1)}, u32[]{:S(2)}, u32[]{:S(2)}) collective-permute-start(bf16[4,64,128]{2,1,0:T(8,128)(2,1)S(1)} %pad_maximum_fusion.1.u0), channel_id=1, source_target_pairs={{4,0},{5,1},{6,2},{7,3},{8,4},{9,5},{10,6},{11,7},{12,8},{13,9},{1... | collective-permute-start | bytes 196616 | tf_op jit(solution)/shard_map/ppermute | solution.py:42
  21.2 6.2 %collective-permute-start.8 = (bf16[48,2176]{1,0:T(8,128)(2,1)S(1)}, bf16[48,2176]{1,0:T(8,128)(2,1)S(1)}, u32[]{:S(2)}, u32[]{:S(2)}) collective-permute-start(bf16[48,2176]{1,0:T(8,128)(2,1)S(1)} %shard_map.85), channel_id=1, source_target_pairs={{128,0},{33,1},{130,2},{35,3},{132,4},{37,5},{134,6},{39,7},{136,8... | collective-permute-start | bytes 626696 | tf_op jit(solution)/shard_map/ppermute | solution.py:42
  24.0 6.2 %collective-permute-start.7 = (bf16[48,2176]{1,0:T(8,128)(2,1)S(1)}, bf16[48,2176]{1,0:T(8,128)(2,1)S(1)}, u32[]{:S(2)}, u32[]{:S(2)}) collective-permute-start(bf16[48,2176]{1,0:T(8,128)(2,1)S(1)} %shard_map.85), channel_id=1, source_target_pairs={{192,0},{49,1},{194,2},{51,3},{196,4},{53,5},{198,6},{55,7},{200,8... | collective-permute-start | bytes 626696 | tf_op jit(solution)/shard_map/ppermute | solution.py:42
  24.4 5.8 %collective-permute-start.6 = (bf16[48,2176]{1,0:T(8,128)(2,1)S(1)}, bf16[48,2176]{1,0:T(8,128)(2,1)S(1)}, u32[]{:S(2)}, u32[]{:S(2)}) collective-permute-start(bf16[48,2176]{1,0:T(8,128)(2,1)S(1)} %shard_map.85), channel_id=1, source_target_pairs={{64,0},{17,1},{66,2},{19,3},{68,4},{21,5},{70,6},{23,7},{72,8},{25... | collective-permute-start | bytes 626696 | tf_op jit(solution)/shard_map/ppermute | solution.py:42
  30.4 19.6 %collective-permute-start.11 = (bf16[4,48,2176]{2,1,0:T(8,128)(2,1)S(1)}, bf16[4,48,2176]{2,1,0:T(8,128)(2,1)S(1)}, u32[]{:S(2)}, u32[]{:S(2)}) collective-permute-start(bf16[4,48,2176]{2,1,0:T(8,128)(2,1)S(1)} %pad_maximum_fusion.a0), channel_id=1, source_target_pairs={{32,0},{129,1},{34,2},{131,3},{36,4},{133,5},{38,6},{135,7},{40,8}... | collective-permute-start | bytes 2506760 | tf_op jit(solution)/shard_map/ppermute | solution.py:42
  33.2 24.1 %collective-permute-start.10 = (bf16[4,48,2176]{2,1,0:T(8,128)(2,1)S(1)}, bf16[4,48,2176]{2,1,0:T(8,128)(2,1)S(1)}, u32[]{:S(2)}, u32[]{:S(2)}) collective-permute-start(bf16[4,48,2176]{2,1,0:T(8,128)(2,1)S(1)} %pad_maximum_fusion.a0), channel_id=1, source_target_pairs={{48,0},{193,1},{50,2},{195,3},{52,4},{197,5},{54,6},{199,7},{56,8}... | collective-permute-start | bytes 2506760 | tf_op jit(solution)/shard_map/ppermute | solution.py:42
  33.8 32.4 %collective-permute-start.9 = (bf16[4,48,2176]{2,1,0:T(8,128)(2,1)S(1)}, bf16[4,48,2176]{2,1,0:T(8,128)(2,1)S(1)}, u32[]{:S(2)}, u32[]{:S(2)}) collective-permute-start(bf16[4,48,2176]{2,1,0:T(8,128)(2,1)S(1)} %pad_maximum_fusion.a0), channel_id=1, source_target_pairs={{16,0},{65,1},{18,2},{67,3},{20,4},{69,5},{22,6},{71,7},{24,8},{73... | collective-permute-start | bytes 2506760 | tf_op jit(solution)/shard_map/ppermute | solution.py:42
  35.9 30.5 %collective-permute-start.12 = (bf16[4,48,2176]{2,1,0:T(8,128)(2,1)S(1)}, bf16[4,48,2176]{2,1,0:T(8,128)(2,1)S(1)}, u32[]{:S(2)}, u32[]{:S(2)}) collective-permute-start(bf16[4,48,2176]{2,1,0:T(8,128)(2,1)S(1)} %pad_maximum_fusion.a0), channel_id=1, source_target_pairs={{1,0},{0,1},{3,2},{2,3},{5,4},{4,5},{7,6},{6,7},{9,8},{8,9},{11,10... | collective-permute-start | bytes 2506760 | tf_op jit(solution)/shard_map/ppermute | solution.py:42
  49.9 16.5 %collective-permute-start.15 = (bf16[4,48,2176]{2,1,0:T(8,128)(2,1)S(1)}, bf16[4,48,2176]{2,1,0:T(8,128)(2,1)S(1)}, u32[]{:S(2)}, u32[]{:S(2)}) collective-permute-start(bf16[4,48,2176]{2,1,0:T(8,128)(2,1)S(1)} %collective-permute-done.11.a3), channel_id=1, source_target_pairs={{1,0},{0,1},{3,2},{2,3},{5,4},{4,5},{7,6},{6,7},{9,8},{8,9},{11,10... | collective-permute-start | bytes 2506760 | tf_op jit(solution)/shard_map/ppermute | solution.py:42
  57.3 10.8 %collective-permute-start.14 = (bf16[4,48,2176]{2,1,0:T(8,128)(2,1)S(1)}, bf16[4,48,2176]{2,1,0:T(8,128)(2,1)S(1)}, u32[]{:S(2)}, u32[]{:S(2)}) collective-permute-start(bf16[4,48,2176]{2,1,0:T(8,128)(2,1)S(1)} %collective-permute-done.10.a2), channel_id=1, source_target_pairs={{1,0},{0,1},{3,2},{2,3},{5,4},{4,5},{7,6},{6,7},{9,8},{8,9},{11,10... | collective-permute-start | bytes 2506760 | tf_op jit(solution)/shard_map/ppermute | solution.py:42
  83.4 5.6 %collective-permute-start.21 = (f32[3,8,128]{2,1,0:T(8,128)S(1)}, f32[3,8,128]{2,1,0:T(8,128)S(1)}, u32[]{:S(2)}, u32[]{:S(2)}) collective-permute-start(f32[3,8,128]{2,1,0:T(8,128)S(1)} %shard_map.87.a), channel_id=1, source_target_pairs={{12,0},{13,1},{14,2},{15,3},{0,4},{1,5},{2,6},{3,7},{4,8},{5,9},{6... | collective-permute-start | bytes 36872 | tf_op jit(solution)/shard_map/ppermute | solution.py:42
  83.5 5.5 %collective-permute-start.20 = (f32[3,8,128]{2,1,0:T(8,128)S(1)}, f32[3,8,128]{2,1,0:T(8,128)S(1)}, u32[]{:S(2)}, u32[]{:S(2)}) collective-permute-start(f32[3,8,128]{2,1,0:T(8,128)S(1)} %shard_map.87.a), channel_id=1, source_target_pairs={{4,0},{5,1},{6,2},{7,3},{8,4},{9,5},{10,6},{11,7},{12,8},{13,9},{1... | collective-permute-start | bytes 36872 | tf_op jit(solution)/shard_map/ppermute | solution.py:42
  87.0 6.5 %collective-permute-start.19 = (f32[3,8,128]{2,1,0:T(8,128)S(1)}, f32[3,8,128]{2,1,0:T(8,128)S(1)}, u32[]{:S(2)}, u32[]{:S(2)}) collective-permute-start(f32[3,8,128]{2,1,0:T(8,128)S(1)} %shard_map.87.a), channel_id=1, source_target_pairs={{8,0},{9,1},{10,2},{11,3},{12,4},{13,5},{14,6},{15,7},{0,8},{1,9},... | collective-permute-start | bytes 36872 | tf_op jit(solution)/shard_map/ppermute | solution.py:42
  93.5 4.4 %collective-permute-start.24 = (f32[3,8,128]{2,1,0:T(8,128)S(1)}, f32[3,8,128]{2,1,0:T(8,128)S(1)}, u32[]{:S(2)}, u32[]{:S(2)}) collective-permute-start(f32[3,8,128]{2,1,0:T(8,128)S(1)} %shard_map.88.a), channel_id=1, source_target_pairs={{192,0},{193,1},{194,2},{195,3},{196,4},{197,5},{198,6},{199,7},{2... | collective-permute-start | bytes 36872 | tf_op jit(solution)/shard_map/ppermute | solution.py:42
  93.9 4.1 %collective-permute-start.23 = (f32[3,8,128]{2,1,0:T(8,128)S(1)}, f32[3,8,128]{2,1,0:T(8,128)S(1)}, u32[]{:S(2)}, u32[]{:S(2)}) collective-permute-start(f32[3,8,128]{2,1,0:T(8,128)S(1)} %shard_map.88.a), channel_id=1, source_target_pairs={{64,0},{65,1},{66,2},{67,3},{68,4},{69,5},{70,6},{71,7},{72,8},{73... | collective-permute-start | bytes 36872 | tf_op jit(solution)/shard_map/ppermute | solution.py:42
  96.8 4.0 %collective-permute-start.22 = (f32[3,8,128]{2,1,0:T(8,128)S(1)}, f32[3,8,128]{2,1,0:T(8,128)S(1)}, u32[]{:S(2)}, u32[]{:S(2)}) collective-permute-start(f32[3,8,128]{2,1,0:T(8,128)S(1)} %shard_map.88.a), channel_id=1, source_target_pairs={{128,0},{129,1},{130,2},{131,3},{132,4},{133,5},{134,6},{135,7},{1... | collective-permute-start | bytes 36872 | tf_op jit(solution)/shard_map/ppermute | solution.py:42
  100.9 13.7 %collective-permute-start.27 = (f32[3,8,128]{2,1,0:T(8,128)S(1)}, f32[3,8,128]{2,1,0:T(8,128)S(1)}, u32[]{:S(2)}, u32[]{:S(2)}) collective-permute-start(f32[3,8,128]{2,1,0:T(8,128)S(1)} %shard_map.89.a), channel_id=1, source_target_pairs={{48,0},{49,1},{50,2},{51,3},{52,4},{53,5},{54,6},{55,7},{56,8},{57... | collective-permute-start | bytes 36872 | tf_op jit(solution)/shard_map/ppermute | solution.py:42
  128.4 16.1 %collective-permute-start.28 = (bf16[768,2048]{1,0:T(8,128)(2,1)}, bf16[768,2048]{1,0:T(8,128)(2,1)}, u32[]{:S(2)}, u32[]{:S(2)}) collective-permute-start(bf16[768,2048]{1,0:T(8,128)(2,1)} %get-tuple-element.29), channel_id=1, source_target_pairs={{1,0},{0,1},{3,2},{2,3},{5,4},{4,5},{7,6},{6,7},{9,8},{8,9},{11,10... | collective-permute-start | bytes 9437192 | tf_op jit(solution)/shard_map/ppermute | solution.py:42
  156.9 12.6 %collective-permute-start.29 = (bf16[4,48,2048]{2,1,0:T(8,128)(2,1)}, bf16[4,48,2048]{2,1,0:T(8,128)(2,1)S(1)}, u32[]{:S(2)}, u32[]{:S(2)}) collective-permute-start(bf16[4,48,2048]{2,1,0:T(8,128)(2,1)} %get-tuple-element.31), channel_id=1, source_target_pairs={{48,0},{193,1},{50,2},{195,3},{52,4},{197,5},{54,6},{199,7},{56,8}... | collective-permute-start | bytes 2359304 | tf_op jit(solution)/shard_map/ppermute | solution.py:42
  156.9 20.4 %collective-permute-start.30 = (bf16[4,48,2048]{2,1,0:T(8,128)(2,1)}, bf16[4,48,2048]{2,1,0:T(8,128)(2,1)S(1)}, u32[]{:S(2)}, u32[]{:S(2)}) collective-permute-start(bf16[4,48,2048]{2,1,0:T(8,128)(2,1)} %get-tuple-element.32), channel_id=1, source_target_pairs={{16,0},{65,1},{18,2},{67,3},{20,4},{69,5},{22,6},{71,7},{24,8},{73... | collective-permute-start | bytes 2359304 | tf_op jit(solution)/shard_map/ppermute | solution.py:42
  159.6 18.2 %collective-permute-start.31 = (bf16[4,48,2048]{2,1,0:T(8,128)(2,1)}, bf16[4,48,2048]{2,1,0:T(8,128)(2,1)S(1)}, u32[]{:S(2)}, u32[]{:S(2)}) collective-permute-start(bf16[4,48,2048]{2,1,0:T(8,128)(2,1)} %get-tuple-element.33), channel_id=1, source_target_pairs={{32,0},{129,1},{34,2},{131,3},{36,4},{133,5},{38,6},{135,7},{40,8}... | collective-permute-start | bytes 2359304 | tf_op jit(solution)/shard_map/ppermute | solution.py:42
  179.5 6.1 %collective-permute-start.32 = (bf16[48,2048]{1,0:T(8,128)(2,1)S(1)}, bf16[48,2048]{1,0:T(8,128)(2,1)S(1)}, u32[]{:S(2)}, u32[]{:S(2)}) collective-permute-start(bf16[48,2048]{1,0:T(8,128)(2,1)S(1)} %get-tuple-element.35), channel_id=1, source_target_pairs={{192,0},{49,1},{194,2},{51,3},{196,4},{53,5},{198,6},{55,7},{200,8... | collective-permute-start | bytes 589832 | tf_op jit(solution)/shard_map/ppermute | solution.py:42
  180.1 6.8 %collective-permute-start.33 = (bf16[48,2048]{1,0:T(8,128)(2,1)S(1)}, bf16[48,2048]{1,0:T(8,128)(2,1)S(1)}, u32[]{:S(2)}, u32[]{:S(2)}) collective-permute-start(bf16[48,2048]{1,0:T(8,128)(2,1)S(1)} %get-tuple-element.36), channel_id=1, source_target_pairs={{64,0},{17,1},{66,2},{19,3},{68,4},{21,5},{70,6},{23,7},{72,8},{25... | collective-permute-start | bytes 589832 | tf_op jit(solution)/shard_map/ppermute | solution.py:42
  182.2 6.3 %collective-permute-start.34 = (bf16[48,2048]{1,0:T(8,128)(2,1)S(1)}, bf16[48,2048]{1,0:T(8,128)(2,1)S(1)}, u32[]{:S(2)}, u32[]{:S(2)}) collective-permute-start(bf16[48,2048]{1,0:T(8,128)(2,1)S(1)} %get-tuple-element.37), channel_id=1, source_target_pairs={{128,0},{33,1},{130,2},{35,3},{132,4},{37,5},{134,6},{39,7},{136,8... | collective-permute-start | bytes 589832 | tf_op jit(solution)/shard_map/ppermute | solution.py:42
  189.3 5.2 %collective-permute-start.35 = (bf16[4,48,128]{2,1,0:T(8,128)(2,1)S(1)}, bf16[4,48,128]{2,1,0:T(8,128)(2,1)S(1)}, u32[]{:S(2)}, u32[]{:S(2)}) collective-permute-start(bf16[4,48,128]{2,1,0:T(8,128)(2,1)S(1)} %get-tuple-element.39), channel_id=1, source_target_pairs={{12,0},{13,1},{14,2},{15,3},{0,4},{1,5},{2,6},{3,7},{4,8},{5,9},{6... | collective-permute-start | bytes 147464 | tf_op jit(solution)/shard_map/ppermute | solution.py:42
  189.4 5.1 %collective-permute-start.36 = (bf16[4,48,128]{2,1,0:T(8,128)(2,1)S(1)}, bf16[4,48,128]{2,1,0:T(8,128)(2,1)S(1)}, u32[]{:S(2)}, u32[]{:S(2)}) collective-permute-start(bf16[4,48,128]{2,1,0:T(8,128)(2,1)S(1)} %get-tuple-element.40), channel_id=1, source_target_pairs={{4,0},{5,1},{6,2},{7,3},{8,4},{9,5},{10,6},{11,7},{12,8},{13,9},{1... | collective-permute-start | bytes 147464 | tf_op jit(solution)/shard_map/ppermute | solution.py:42
  193.0 7.4 %collective-permute-start.37 = (bf16[4,48,128]{2,1,0:T(8,128)(2,1)S(1)}, bf16[4,48,128]{2,1,0:T(8,128)(2,1)S(1)}, u32[]{:S(2)}, u32[]{:S(2)}) collective-permute-start(bf16[4,48,128]{2,1,0:T(8,128)(2,1)S(1)} %get-tuple-element.41), channel_id=1, source_target_pairs={{8,0},{9,1},{10,2},{11,3},{12,4},{13,5},{14,6},{15,7},{0,8},{1,9},... | collective-permute-start | bytes 147464 | tf_op jit(solution)/shard_map/ppermute | solution.py:42
  200.4 17.3 %collective-permute-start.38 = (bf16[48,128]{1,0:T(8,128)(2,1)S(1)}, bf16[48,128]{1,0:T(8,128)(2,1)S(1)}, u32[]{:S(2)}, u32[]{:S(2)}) collective-permute-start(bf16[48,128]{1,0:T(8,128)(2,1)S(1)} %get-tuple-element.43), channel_id=1, source_target_pairs={{2,0},{3,1},{0,2},{1,3},{6,4},{7,5},{4,6},{5,7},{10,8},{11,9},{8,1... | collective-permute-start | bytes 36872 | tf_op jit(solution)/shard_map/ppermute | solution.py:42
  212.8 4.9 %collective-permute-start.39 = (bf16[48,128]{1,0:T(8,128)(2,1)S(1)}, bf16[48,128]{1,0:T(8,128)(2,1)S(1)}, u32[]{:S(2)}, u32[]{:S(2)}) collective-permute-start(bf16[48,128]{1,0:T(8,128)(2,1)S(1)} %get-tuple-element.44), channel_id=1, source_target_pairs={{1,0},{0,1},{3,2},{2,3},{5,4},{4,5},{7,6},{6,7},{9,8},{8,9},{11,10... | collective-permute-start | bytes 36872 | tf_op jit(solution)/shard_map/ppermute | solution.py:42
  (19 other events, 301.3 us)
